TPU v7x, 32 devices: a whole 2x2x4 slice. The times are simulated.
32 devices in a mesh: fsdp: 4 (over z), ctx: 4 (over y, core), tp: 2 (over x).
Axes of the slice: x: 2, y: 2, z: 4, core: 2. Of those that a mesh axis runs over, the one named last changes fastest.
Arguments:
- block_input: bfloat16 [4, 1024, 1024], P('fsdp', 'ctx'), may hold values from -6 to 6
- input_gain: float32 [1024], replicated, may hold values from 0.5 to 1.5
- gate_proj: bfloat16 [1024, 2048], P('fsdp', 'tp'), may hold values from -0.1875 to 0.1875
- x_proj: bfloat16 [1024, 2048], P('fsdp', 'tp'), may hold values from -0.1875 to 0.1875
- bc_proj: bfloat16 [1024, 256], P('fsdp'), may hold values from -0.1875 to 0.1875
- dt_proj: bfloat16 [1024, 32], P('fsdp', 'tp'), may hold values from -0.1875 to 0.1875
- x_conv: float32 [4, 2048], P(None, 'tp'), may hold values from -3 to 3
- bc_conv: float32 [4, 256], replicated, may hold values from -3 to 3
- dt_bias: float32 [32], P('tp'), may hold values from -2 to 1
- a_log: float32 [32], P('tp'), may hold values from -11 to -2
- skip_gain: float32 [32], P('tp'), may hold values from 0.5 to 1.5
- gated_gain: float32 [2048], P('tp'), may hold values from 0.5 to 1.5
- out_proj: bfloat16 [2048, 1024], P('tp', 'fsdp'), may hold values from -0.125 to 0.125
- cotangent: bfloat16 [4, 1024, 1024], P('fsdp', 'ctx'), may hold values from -6 to 6
Outputs:
- block_output: bfloat16 [4, 1024, 1024], P('fsdp', 'ctx')
- input_grad: float32 [4, 1024, 1024], P('fsdp', 'ctx')
- grad_input_gain: float32 [1024], replicated
- grad_gate_proj: float32 [1024, 2048], P('fsdp', 'tp')
- grad_x_proj: float32 [1024, 2048], P('fsdp', 'tp')
- grad_bc_proj: float32 [1024, 256], P('fsdp')
- grad_dt_proj: float32 [1024, 32], P('fsdp', 'tp')
- grad_x_conv: float32 [4, 2048], P(None, 'tp')
- grad_bc_conv: float32 [4, 256], replicated
- grad_dt_bias: float32 [32], P('tp')
- grad_a_log: float32 [32], P('tp')
- grad_skip_gain: float32 [32], P('tp')
- grad_gated_gain: float32 [2048], P('tp')
- grad_out_proj: float32 [2048, 1024], P('tp', 'fsdp')
All inputs are finite; a program needn't handle non-finite values.
Results may differ from a plain program's by a relative error of at most 0.0098.
Values may be sent and summed in bfloat16 or wider, within the bound.
No kernel may reach another device: no remote copies, remote signals or barrier semaphores. Data moves between devices by JAX's collectives and lax.ppermute only.
A program may use at most 128 MiB of HBM per device.

v0:
```python
import jax
import jax.numpy as jnp
from jax import lax
from jax.sharding import PartitionSpec as P

EPSILON = 1e-05
FINE = lax.Precision.HIGHEST


def from_behind(block, axis, distance):
    devices = range(lax.axis_size(axis))
    route = [(i - distance, i) for i in devices if i - distance in devices]
    return lax.ppermute(block, axis, route)


def carried_in(part, axis, combine, identity, reverse):
    count = lax.axis_size(axis)
    place = lax.axis_index(axis)
    ahead = count - 1 - place if reverse else place
    gathered = jax.tree.map(lambda a: lax.all_gather(a, axis), part)
    state = jax.tree.map(lambda a, e: jnp.zeros_like(a) + jnp.asarray(e, a.dtype), part, identity)

    def one(lap, state):
        source = count - 1 - lap if reverse else lap
        return combine(
            state, jax.tree.map(lambda a: lax.dynamic_index_in_dim(a, source, 0, False), gathered)
        )

    return lax.fori_loop(0, ahead, one, state)


def combine_states(earlier, later):
    return (earlier[0] * later[0], earlier[1] * later[0][:, :, None, None] + later[1])


def silu_slope(values):
    sigmoid_value = jax.nn.sigmoid(values)
    return sigmoid_value * (1.0 + values * (1.0 - sigmoid_value))


def block_local(x_heads, b_rows, c_rows, step_size, log_decay):
    cumulative = jnp.cumsum(log_decay, axis=2)
    log_gaps = cumulative[:, :, :, None] - cumulative[:, :, None, :]
    length = log_decay.shape[2]
    causal = jnp.tril(jnp.ones((length, length), jnp.bool_))
    decays = jnp.where(causal, jnp.exp(jnp.where(causal, log_gaps, 0.0)), 0.0)
    scores = jnp.einsum("btn,bsn->bts", c_rows, b_rows, precision=FINE)
    weights = decays * scores[:, None, :, :] * step_size[:, :, None, :]
    within = jnp.einsum("bhts,bshp->bthp", weights, x_heads, precision=FINE)
    tail_decay = jnp.exp(cumulative[:, :, -1:] - cumulative) * step_size
    summary = jnp.einsum("bhs,bshp,bsn->bhpn", tail_decay, x_heads, b_rows, precision=FINE)
    return (within, summary, jnp.exp(cumulative[:, :, -1]))


def block_carry(c_rows, log_decay, state_in):
    cumulative = jnp.cumsum(log_decay, axis=2)
    carried = jnp.einsum("btn,bhpn->bthp", c_rows, state_in, precision=FINE)
    return jnp.exp(cumulative).transpose(0, 2, 1)[:, :, :, None] * carried


def back_product(grad_low, weight):
    return lax.dot_general(
        grad_low, weight, (((1,), (1,)), ((), ())), preferred_element_type=jnp.float32
    )


def on_device(
    block_input,
    input_gain,
    gate_proj,
    x_proj,
    bc_proj,
    dt_proj,
    x_conv,
    bc_conv,
    dt_bias,
    a_log,
    skip_gain,
    gated_gain,
    out_proj,
    cotangent,
):
    seqs_here, length, model_width = block_input.shape
    row_count = seqs_here * length
    inner_here = gate_proj.shape[1]
    heads_here = dt_proj.shape[1]
    head_size = inner_here // heads_here
    state_size = bc_proj.shape[1] // 2
    tap_count = x_conv.shape[0]
    full_inner = inner_here * lax.axis_size("tp")
    full_gate, full_x, full_bc, full_dt, full_out = (
        lax.all_gather(gate_proj, "fsdp", axis=0, tiled=True),
        lax.all_gather(x_proj, "fsdp", axis=0, tiled=True),
        lax.all_gather(bc_proj, "fsdp", axis=0, tiled=True),
        lax.all_gather(dt_proj, "fsdp", axis=0, tiled=True),
        lax.all_gather(out_proj, "fsdp", axis=1, tiled=True),
    )
    residual = block_input.astype(jnp.float32)
    in_scale = lax.rsqrt(jnp.mean(residual * residual, axis=-1, keepdims=True) + EPSILON)
    normed_low = (
        (residual * in_scale * input_gain).astype(jnp.bfloat16).reshape(row_count, model_width)
    )
    gate_input = jnp.dot(normed_low, full_gate, preferred_element_type=jnp.float32).reshape(
        seqs_here, length, inner_here
    )
    x_input = jnp.dot(normed_low, full_x, preferred_element_type=jnp.float32).reshape(
        seqs_here, length, inner_here
    )
    bc_input = jnp.dot(normed_low, full_bc, preferred_element_type=jnp.float32).reshape(
        seqs_here, length, 2 * state_size
    )
    dt_input = jnp.dot(normed_low, full_dt, preferred_element_type=jnp.float32).reshape(
        seqs_here, length, heads_here
    )
    conv_input = jnp.concatenate([x_input, bc_input], axis=-1)
    conv_taps = jnp.concatenate([x_conv, bc_conv], axis=-1)
    edge_rows = from_behind(conv_input[:, length - tap_count + 1 :, :], "ctx", 1)
    padded = jnp.concatenate([edge_rows, conv_input], axis=1)
    conv_out = jnp.zeros_like(conv_input)
    for offset in range(tap_count):
        conv_out = conv_out + conv_taps[offset] * padded[:, offset : offset + length, :]
    activated = jax.nn.silu(conv_out)
    x_heads = activated[:, :, :inner_here].reshape(seqs_here, length, heads_here, head_size)
    b_rows = activated[:, :, inner_here : inner_here + state_size]
    c_rows = activated[:, :, inner_here + state_size :]
    pre_step = dt_input.transpose(0, 2, 1) + dt_bias[None, :, None]
    step_size = jax.nn.softplus(pre_step)
    decay_rates = jnp.exp(a_log)[None, :, None]
    log_decay = -decay_rates * step_size
    (within, summary, total_decay), local_back = jax.vjp(
        block_local, x_heads, b_rows, c_rows, step_size, log_decay
    )
    identity = (jnp.ones_like(total_decay), jnp.zeros_like(summary))
    state_in = carried_in((total_decay, summary), "ctx", combine_states, identity, False)[1]
    carried, carry_back = jax.vjp(block_carry, c_rows, log_decay, state_in)
    mixed_heads = within + carried + skip_gain[None, None, :, None] * x_heads
    mixed_flat = mixed_heads.reshape(seqs_here, length, inner_here)
    gate_act = jax.nn.silu(gate_input)
    gated_rows = mixed_flat * gate_act
    square_sum = lax.psum(jnp.sum(gated_rows * gated_rows, axis=-1), "tp")
    out_scale = lax.rsqrt(square_sum / full_inner + EPSILON)[:, :, None]
    normed_out = (
        (gated_rows * out_scale * gated_gain).astype(jnp.bfloat16).reshape(row_count, inner_here)
    )
    branch_sum = lax.psum(jnp.dot(normed_out, full_out, preferred_element_type=jnp.float32), "tp")
    block_output = (residual + branch_sum.reshape(seqs_here, length, model_width)).astype(
        jnp.bfloat16
    )
    cot_rows = cotangent.reshape(row_count, model_width)
    grad_out_w = lax.dot_general(
        normed_out, cot_rows, (((0,), (0,)), ((), ())), preferred_element_type=jnp.float32
    )
    d_normed_low = back_product(cot_rows, full_out).astype(jnp.bfloat16)
    d_normed_out = d_normed_low.astype(jnp.float32).reshape(seqs_here, length, inner_here)
    grad_gated_gain = jnp.sum(d_normed_out * gated_rows * out_scale, axis=(0, 1))
    cross_sum = lax.psum(jnp.sum(d_normed_out * gated_gain * gated_rows, axis=-1), "tp")
    d_gated = (
        out_scale * gated_gain * d_normed_out
        - gated_rows * (out_scale**3 / full_inner) * cross_sum[:, :, None]
    )
    d_mixed = (d_gated * gate_act).reshape(seqs_here, length, heads_here, head_size)
    d_gate_low = (
        (d_gated * mixed_flat * silu_slope(gate_input))
        .astype(jnp.bfloat16)
        .reshape(row_count, inner_here)
    )
    grad_skip_gain = jnp.sum(d_mixed * x_heads, axis=(0, 1, 3))
    d_c_carry, d_decay_carry, state_grad = carry_back(d_mixed)
    later_grad = carried_in((total_decay, state_grad), "ctx", combine_states, identity, True)[1]
    d_total = jnp.sum(later_grad * state_in, axis=(2, 3))
    d_x_heads, d_b_rows, d_c_rows, d_step, d_log_decay = local_back((d_mixed, later_grad, d_total))
    d_x_heads = d_x_heads + skip_gain[None, None, :, None] * d_mixed
    d_c_rows = d_c_rows + d_c_carry
    d_log_decay = d_log_decay + d_decay_carry
    grad_a_log = jnp.sum(d_log_decay * log_decay, axis=(0, 2))
    d_pre = (d_step - decay_rates * d_log_decay) * jax.nn.sigmoid(pre_step)
    grad_dt_bias = jnp.sum(d_pre, axis=(0, 2))
    d_dt_low = d_pre.transpose(0, 2, 1).astype(jnp.bfloat16).reshape(row_count, heads_here)
    d_activated = jnp.concatenate(
        [d_x_heads.reshape(seqs_here, length, inner_here), d_b_rows, d_c_rows], axis=-1
    )
    d_conv_out = d_activated * silu_slope(conv_out)
    d_padded = jnp.zeros_like(padded)
    tap_grads = []
    for offset in range(tap_count):
        tap_grads.append(jnp.sum(d_conv_out * padded[:, offset : offset + length, :], axis=(0, 1)))
        d_padded = d_padded.at[:, offset : offset + length, :].add(conv_taps[offset] * d_conv_out)
    grad_taps = jnp.stack(tap_grads)
    edge_grad = from_behind(d_padded[:, : tap_count - 1, :], "ctx", -1)
    d_conv_input = d_padded[:, tap_count - 1 :, :] + jnp.pad(
        edge_grad, ((0, 0), (length - tap_count + 1, 0), (0, 0))
    )
    d_x_low = d_conv_input[:, :, :inner_here].astype(jnp.bfloat16).reshape(row_count, inner_here)
    partial_normed = (
        back_product(d_gate_low, full_gate)
        + back_product(d_x_low, full_x)
        + back_product(d_dt_low, full_dt)
    )
    summed_normed, summed_bc, grad_bc_conv = lax.psum(
        (
            partial_normed,
            d_conv_input[:, :, inner_here:].reshape(row_count, 2 * state_size),
            grad_taps[:, inner_here:],
        ),
        "tp",
    )
    d_bc_low = summed_bc.astype(jnp.bfloat16)
    d_normed = (summed_normed + back_product(d_bc_low, full_bc)).reshape(
        seqs_here, length, model_width
    )

    def weight_grad(grad_low):
        return lax.dot_general(
            normed_low, grad_low, (((0,), (0,)), ((), ())), preferred_element_type=jnp.float32
        )

    weight_grads = (
        weight_grad(d_gate_low),
        weight_grad(d_x_low),
        weight_grad(d_bc_low),
        weight_grad(d_dt_low),
        grad_out_w,
    )
    grad_input_gain = jnp.sum(d_normed * residual * in_scale, axis=(0, 1))
    d_scaled = d_normed * input_gain
    input_grad = (
        cotangent.astype(jnp.float32)
        + in_scale * d_scaled
        - residual
        * (in_scale**3 / model_width)
        * jnp.sum(d_scaled * residual, axis=-1, keepdims=True)
    )
    sectioned = (
        lax.psum_scatter(weight_grads[0], "fsdp", scatter_dimension=0, tiled=True),
        lax.psum_scatter(weight_grads[1], "fsdp", scatter_dimension=0, tiled=True),
        lax.psum_scatter(weight_grads[2], "fsdp", scatter_dimension=0, tiled=True),
        lax.psum_scatter(weight_grads[3], "fsdp", scatter_dimension=0, tiled=True),
        lax.psum_scatter(weight_grads[4], "fsdp", scatter_dimension=1, tiled=True),
    )
    owned_rows = (
        lax.psum_scatter(sectioned[0], "ctx", scatter_dimension=0, tiled=True),
        lax.psum_scatter(sectioned[1], "ctx", scatter_dimension=0, tiled=True),
        lax.psum_scatter(sectioned[2], "ctx", scatter_dimension=0, tiled=True),
        lax.psum_scatter(sectioned[3], "ctx", scatter_dimension=0, tiled=True),
        lax.psum_scatter(sectioned[4], "ctx", scatter_dimension=1, tiled=True),
    )
    grad_gate_proj, grad_x_proj, grad_bc_proj, grad_dt_proj, grad_out_proj = (
        lax.all_gather(owned_rows[0], "ctx", axis=0, tiled=True),
        lax.all_gather(owned_rows[1], "ctx", axis=0, tiled=True),
        lax.all_gather(owned_rows[2], "ctx", axis=0, tiled=True),
        lax.all_gather(owned_rows[3], "ctx", axis=0, tiled=True),
        lax.all_gather(owned_rows[4], "ctx", axis=1, tiled=True),
    )
    small_totals = lax.psum(
        (
            grad_input_gain,
            grad_taps[:, :inner_here],
            grad_bc_conv,
            grad_dt_bias,
            grad_a_log,
            grad_skip_gain,
            grad_gated_gain,
        ),
        ("fsdp", "ctx"),
    )
    return (
        block_output,
        input_grad,
        small_totals[0],
        grad_gate_proj,
        grad_x_proj,
        grad_bc_proj,
        grad_dt_proj,
        small_totals[1],
        small_totals[2],
        small_totals[3],
        small_totals[4],
        small_totals[5],
        small_totals[6],
        grad_out_proj,
    )


def solution(mesh):
    in_specs = (
        P("fsdp", "ctx", None),
        P(),
        P("fsdp", "tp"),
        P("fsdp", "tp"),
        P("fsdp", None),
        P("fsdp", "tp"),
        P(None, "tp"),
        P(),
        P("tp"),
        P("tp"),
        P("tp"),
        P("tp"),
        P("tp", "fsdp"),
        P("fsdp", "ctx", None),
    )
    out_specs = (
        P("fsdp", "ctx", None),
        P("fsdp", "ctx", None),
        P(),
        P("fsdp", "tp"),
        P("fsdp", "tp"),
        P("fsdp", None),
        P("fsdp", "tp"),
        P(None, "tp"),
        P(),
        P("tp"),
        P("tp"),
        P("tp"),
        P("tp"),
        P("tp", "fsdp"),
    )
    return jax.shard_map(
        on_device, mesh=mesh, in_specs=in_specs, out_specs=out_specs, check_vma=False
    )
```

profile of v0, /device:TPU:0, one launch (start us, length us, event | category | flops | bytes accessed | tf_op | source)
XLA Modules:
  0.0 786.6 jit_solution(12926951627118034505)
XLA Ops:
  8.0 15.0 %all_gather.50 = bf16[1024,16]{0,1:T(8,128)(2,1)S(1)} all-gather(bf16[256,16]{0,1:T(8,128)(2,1)} %param.31), channel_id=1, replica_groups=mesh['fsdp'=4,'ctx'=4,'tp'=2] {'fsdp'}, dimensions={0}, use_global_device_ids=true | all-gather | bytes 40960 | tf_op jit(solution)/shard_map/all_gather | solution.py:95
  29.3 22.7 %all_gather.49 = bf16[1024,256]{1,0:T(8,128)(2,1)S(1)} all-gather(bf16[256,256]{1,0:T(8,128)(2,1)S(1)} %copy-done.44), channel_id=1, replica_groups=mesh['fsdp'=4,'ctx'=4,'tp'=2] {'fsdp'}, dimensions={0}, use_global_device_ids=true | all-gather | bytes 655360 | tf_op jit(solution)/shard_map/all_gather | solution.py:94
  54.0 12.6 %all-gather.13.cloned.1.call-done = bf16[1024,1024]{1,0:T(8,128)(2,1)} async-done(((bf16[256,1024]{1,0:T(8,128)(2,1)}), bf16[1024,1024]{1,0:T(8,128)(2,1)}) %all-gather.13.cloned.1.call-update) | async-done | bytes 2097168 | tf_op jit(solution)/shard_map/all_gather | solution.py:93
  77.2 3.0 fusion.62
  83.0 7.0 all-gather
  91.1 2.6 copy.207
  96.4 7.8 all-gather.25.cloned.1.call-done
  106.3 6.0 fusion.36
  112.3 2.6 copy.205
  114.9 36.8 %all-gather.15.cloned.1.call-done = bf16[1024,1024]{1,0:T(8,128)(2,1)} async-done(((bf16[256,1024]{1,0:T(8,128)(2,1)}), bf16[1024,1024]{1,0:T(8,128)(2,1)}) %all-gather.15.cloned.1.call-update) | async-done | bytes 2097168 | tf_op jit(solution)/shard_map/all_gather | solution.py:92
  151.7 3.7 multiply_reduce_fusion.8
  155.4 4.9 psum.91
  160.3 37.8 %all-gather.17.cloned.1.call-done = bf16[1024,1024]{1,0:T(8,128)(2,1)} async-done(((bf16[1024,256]{1,0:T(8,128)(2,1)}), bf16[1024,1024]{1,0:T(8,128)(2,1)}) %all-gather.17.cloned.1.call-update) | async-done | bytes 2097168 | tf_op jit(solution)/shard_map/all_gather | solution.py:96
  198.2 4.0 fusion.49
  202.2 5.4 psum.93
  207.6 2.9 fusion.59
  212.6 2.6 copy.208
  215.3 3.0 fusion.88
  221.5 2.8 fusion.121
  224.3 3.9 fusion.68
  228.3 2.6 copy.211
  231.0 8.6 %fusion.8 = (f32[16,256]{1,0:T(8,128)}, f32[16,256]{1,0:T(8,128)}, f32[16,256]{1,0:T(8,128)}, f32[256,256]{1,0:T(8,128)S(1)}) fusion(f32[16,256]{1,0:T(8,128)S(1)} %copy-done.57, f32[256,256]{1,0:T(8,128)} %fusion.92, f32[16,256]{1,0:T(8,128)S(1)} %copy-done.59, pred[256,256]{1,0:T(8,128)(4,1)} %iota_compare_fusion, f32[16,64,256]{2,1,0:T(8,128)} %bitcast.308, ...), kind=kOutput, calls=%fused_computation.20 | convolution fusion | flops 820957184 | bytes 2768896 | tf_op jit(solution)/shard_map/transpose(jvp(bhts,bshp->bthp))/dot_general | solution.py:49
  244.2 6.0 while.31
  252.7 4.9 fusion.30
  257.6 2.5 copy.216
  260.2 3.1 fusion.42
  263.3 2.6 multiply_reduce_fusion.5
  268.7 4.5 scatter-add.11
  273.2 2.6 slice_add_fusion.1
  275.8 4.4 scatter-add.14
  286.6 2.8 fusion.77
  300.4 12.9 %all-reduce.11 = (bf16[256,256]{1,0:T(8,128)(2,1)S(1)}, f32[4,256]{1,0:T(4,128)}) all-reduce(f32[256,256]{1,0:T(8,128)S(1)} %slice_bitcast_fusion, f32[4,256]{1,0:T(4,128)S(1)} %pad_maximum_fusion.2), channel_id=1, replica_groups=mesh['fsdp'=4,'ctx'=4,'tp'=2] {'tp'}, use_global_device_ids=true, to_apply=%region_24.25 | all-reduce | flops 66560 | bytes 401408 | tf_op jit(solution)/shard_map/psum | solution.py:199
  314.8 3.4 reduce-scatter.15.cloned.1.call-done
  318.3 79.6 %reduce-scatter.29.cloned.1.call-done = f32[1024,256]{1,0:T(8,128)} async-done(((f32[1024,1024]{1,0:T(8,128)}), f32[1024,256]{1,0:T(8,128)}) %reduce-scatter.29.cloned.1.call-update) | async-done | bytes 1048592 | tf_op jit(solution)/shard_map/reduce_scatter | solution.py:238
  400.6 77.0 %reduce-scatter.19.cloned.1.call-done = f32[256,1024]{1,0:T(8,128)} async-done(((f32[1024,1024]{1,0:T(8,128)}), f32[256,1024]{1,0:T(8,128)}) %reduce-scatter.19.cloned.1.call-update) | async-done | bytes 1048592 | tf_op jit(solution)/shard_map/reduce_scatter | solution.py:235
  477.6 3.5 convolution_bitcast_fusion
  483.5 16.5 %reduce-scatter.27.cloned.1.call-done = f32[256,16]{0,1:T(8,128)} async-done(((f32[1024,16]{0,1:T(8,128)}), f32[256,16]{0,1:T(8,128)}) %reduce-scatter.27.cloned.1.call-update) | async-done | bytes 16400 | tf_op jit(solution)/shard_map/reduce_scatter | solution.py:237
  502.9 25.2 %reduce-scatter.23.cloned.1.call-done = f32[256,256]{1,0:T(8,128)} async-done(((f32[1024,256]{1,0:T(8,128)}), f32[256,256]{1,0:T(8,128)}) %reduce-scatter.23.cloned.1.call-update) | async-done | bytes 262160 | tf_op jit(solution)/shard_map/reduce_scatter | solution.py:236
  528.2 26.2 %reduce-scatter.17.cloned.1.call-done = f32[64,1024]{1,0:T(8,128)} async-done(((f32[256,1024]{1,0:T(8,128)}), f32[64,1024]{1,0:T(8,128)}) %reduce-scatter.17.cloned.1.call-update) | async-done | bytes 262160 | tf_op jit(solution)/shard_map/reduce_scatter | solution.py:241
  554.4 27.2 %reduce-scatter.33.cloned.1.call-done = f32[64,1024]{1,0:T(8,128)} async-done(((f32[256,1024]{1,0:T(8,128)}), f32[64,1024]{1,0:T(8,128)}) %reduce-scatter.33.cloned.1.call-update) | async-done | bytes 262160
  581.7 27.6 %reduce-scatter.21.cloned.1.call-done = f32[64,1024]{1,0:T(8,128)} async-done(((f32[256,1024]{1,0:T(8,128)}), f32[64,1024]{1,0:T(8,128)}) %reduce-scatter.21.cloned.1.call-update) | async-done | bytes 262160 | tf_op jit(solution)/shard_map/reduce_scatter | solution.py:242
  609.5 22.1 %reduce-scatter.31.cloned.1.call-done = f32[64,16]{1,0:T(8,128)} async-done(((f32[256,16]{1,0:T(8,128)}), f32[64,16]{1,0:T(8,128)}) %reduce-scatter.31.cloned.1.call-update) | async-done | bytes 4112
  632.5 5.2 all-gather.3
  638.4 59.9 %all-reduce.10.cloned.1.call-done = (f32[1,256,1024]{2,1,0:T(8,128)}, f32[256,1024]{1,0:T(8,128)}) async-done(((f32[1,256,1024]{2,1,0:T(8,128)}, f32[256,1024]{1,0:T(8,128)}), (f32[1,256,1024]{2,1,0:T(8,128)}, f32[256,1024]{1,0:T(8,128)})) %all-reduce.10.cloned.1.call-update) | async-done | bytes 2097168 | tf_op jit(solution)/shard_map/psum | solution.py:145
  700.2 62.2 %all-reduce.4 = (f32[1024]{0:T(1024)}, f32[4,1024]{1,0:T(4,128)}, f32[4,256]{1,0:T(4,128)}, f32[16]{0:T(128)}, f32[16]{0:T(128)}, /*index=5*/f32[16]{0:T(128)}, f32[1024]{0:T(1024)}) all-reduce(f32[1024]{0:T(1024)S(1)} %get-tuple-element.317, f32[4,1024]{1,0:T(4,128)S(1)} %slice.219, ...), channel_id=1, replica_groups=mesh['fsdp'=4,'ctx'=4,'tp'=2] {'fsdp','ctx'}, use_global_device_ids=true, to_apply=%region_27.28 | all-reduce | flops 7216 | bytes 57728 | tf_op jit(solution)/shard_map/psum | solution.py:254
  762.5 2.8 fusion.55
  765.2 7.0 all_gather.60
  772.3 2.6 copy.228
  (303 shorter events, 84.4 us)
Async XLA Ops:
  7.2 59.4 %all-gather.13.cloned.1.call-start = ((), (), s32[]{:S(2)}) async-start(), calls=%async_computation.10 | async-start | bytes 2621440 | tf_op jit(solution)/shard_map/all_gather | solution.py:93
  7.9 96.3 %all-gather.25.cloned.1.call-start = ((), (), s32[]{:S(2)}) async-start(), calls=%async_computation.24 | async-start | bytes 2621440 | tf_op jit(solution)/shard_map/all_gather | solution.py:20
  23.0 6.3 copy-start.44
  26.0 26.7 %copy-start.2 = (bf16[1,256,1024]{2,1,0:T(8,128)(2,1)S(1)}, bf16[1,256,1024]{2,1,0:T(8,128)(2,1)}, u32[]{:S(2)}) copy-start(bf16[1,256,1024]{2,1,0:T(8,128)(2,1)} %param.26) | copy-start | bytes 1572868
  26.1 26.7 %copy-start.37 = (f32[1024]{0:T(1024)S(1)}, f32[1024]{0:T(1024)}, u32[]{:S(2)}) copy-start(f32[1024]{0:T(1024)} %param.27) | copy-start | bytes 12292
  27.6 25.6 %copy-start.33 = (f32[1,16,256]{1,2,0:T(8,128)}, f32[1,16,256]{1,2,0:T(8,128)S(1)}, u32[]{:S(2)}) copy-start(f32[1,16,256]{1,2,0:T(8,128)S(1)} %get-tuple-element.380) | copy-start | bytes 49156
  27.6 25.6 %copy-start.29 = (f32[1,16,256]{1,2,0:T(8,128)}, f32[1,16,256]{1,2,0:T(8,128)S(1)}, u32[]{:S(2)}) copy-start(f32[1,16,256]{1,2,0:T(8,128)S(1)} %get-tuple-element.381) | copy-start | bytes 49156
  29.2 24.0 %copy-start.24 = (f32[1,16,256]{1,2,0:T(8,128)}, f32[1,16,256]{1,2,0:T(8,128)S(1)}, u32[]{:S(2)}) copy-start(f32[1,16,256]{1,2,0:T(8,128)S(1)} %get-tuple-element.365) | copy-start | bytes 49156
  53.2 18.5 %copy-start.21 = (f32[1,256,256]{2,1,0:T(8,128)}, f32[1,256,256]{2,1,0:T(8,128)S(1)}, u32[]{:S(2)}) copy-start(f32[1,256,256]{2,1,0:T(8,128)S(1)} %convolution_bitcast_fusion.3) | copy-start | bytes 786436
  53.2 15.7 %copy-start.65 = (f32[16]{0:T(128)}, f32[16]{0:T(128)S(1)}, u32[]{:S(2)}) copy-start(f32[16]{0:T(128)S(1)} %get-tuple-element.374) | copy-start | bytes 196
  69.0 2.6 collective-permute-start
  77.2 29.0 %copy-start.7 = (f32[1,256,1024]{1,2,0:T(8,128)}, f32[1,256,1024]{1,2,0:T(8,128)S(1)}, u32[]{:S(2)}) copy-start(f32[1,256,1024]{1,2,0:T(8,128)S(1)} %copy.193) | copy-start | bytes 3145732
  80.2 9.8 %copy-start.35 = (f32[256,16]{1,0:T(8,128)S(1)}, f32[256,16]{1,0:T(8,128)}, u32[]{:S(2)}) copy-start(f32[256,16]{1,0:T(8,128)} %get-tuple-element.364) | copy-start | bytes 49156
  80.2 71.5 %all-gather.15.cloned.1.call-start = ((), (), s32[]{:S(2)}) async-start(), calls=%async_computation.11 | async-start | bytes 2621440 | tf_op jit(solution)/shard_map/all_gather | solution.py:92
  80.9 117.2 %all-gather.17.cloned.1.call-start = ((), (), s32[]{:S(2)}) async-start(), calls=%async_computation.12 | async-start | bytes 2621440 | tf_op jit(solution)/shard_map/all_gather | solution.py:96
  81.5 162.7 %all-gather.27.cloned.1.call-start = ((), (), s32[]{:S(2)}) async-start(), calls=%async_computation.25 | async-start | bytes 2621440 | tf_op jit(solution)/shard_map/all_gather | solution.py:20
  104.2 8.1 %copy-start.73 = (f32[4,1,16]{2,1,0:T(1,128)}, f32[4,1,16]{2,1,0:T(1,128)S(1)}, u32[]{:S(2)}) copy-start(f32[4,1,16]{2,1,0:T(1,128)S(1)} %get-tuple-element.621) | copy-start | bytes 772
  114.9 83.2 %copy-start.45 = (f32[1024]{0:T(1024)S(1)}, f32[1024]{0:T(1024)}, u32[]{:S(2)}) copy-start(f32[1024]{0:T(1024)} %param.37) | copy-start | bytes 12292
  155.4 69.0 %copy-start.5 = (f32[256,1024]{1,0:T(8,128)}, f32[256,1024]{1,0:T(8,128)S(1)}, u32[]{:S(2)}) copy-start(f32[256,1024]{1,0:T(8,128)S(1)} %get-tuple-element.363) | copy-start | bytes 3145732
  218.3 99.9 %reduce-scatter.15.cloned.1.call-start = ((), (), s32[]{:S(2)}) async-start(), calls=%async_computation.13 | async-start | bytes 5242880 | tf_op jit(solution)/shard_map/reduce_scatter | solution.py:234
  224.3 173.7 %reduce-scatter.29.cloned.1.call-start = ((), (), s32[]{:S(2)}) async-start(), calls=%async_computation.22 | async-start | bytes 5242880 | tf_op jit(solution)/shard_map/reduce_scatter | solution.py:238
  228.3 249.2 %reduce-scatter.19.cloned.1.call-start = ((), (), s32[]{:S(2)}) async-start(), calls=%async_computation.16 | async-start | bytes 5242880 | tf_op jit(solution)/shard_map/reduce_scatter | solution.py:235
  231.0 10.1 %copy-start.13 = (f32[256,1024]{0,1:T(8,128)S(1)}, f32[256,1024]{0,1:T(8,128)}, u32[]{:S(2)}) copy-start(f32[256,1024]{0,1:T(8,128)} %copy.208) | copy-start | bytes 3145732
  280.9 3.1 collective-permute-start.1
  289.5 210.4 %reduce-scatter.27.cloned.1.call-start = ((), (), s32[]{:S(2)}) async-start(), calls=%async_computation.21 | async-start | bytes 81920 | tf_op jit(solution)/shard_map/reduce_scatter | solution.py:237
  293.1 7.2 copy-start.11
  299.3 15.4 %copy-start.40 = (bf16[1,16,256]{1,2,0:T(8,128)(2,1)}, bf16[1,16,256]{1,2,0:T(8,128)(2,1)S(1)}, u32[]{:S(2)}) copy-start(bf16[1,16,256]{1,2,0:T(8,128)(2,1)S(1)} %get-tuple-element.358) | copy-start | bytes 24580
  300.3 227.8 %reduce-scatter.23.cloned.1.call-start = ((), (), s32[]{:S(2)}) async-start(), calls=%async_computation.19 | async-start | bytes 1310720 | tf_op jit(solution)/shard_map/reduce_scatter | solution.py:236
  314.8 239.6 %reduce-scatter.17.cloned.1.call-start = ((), (), s32[]{:S(2)}) async-start(), calls=%async_computation.14 | async-start | bytes 1310720 | tf_op jit(solution)/shard_map/reduce_scatter | solution.py:241
  318.3 263.3 %reduce-scatter.33.cloned.1.call-start = ((), (), s32[]{:S(2)}) async-start(), calls=%async_computation.27 | async-start | bytes 1310720
  400.5 77.1 %copy-start.6 = (f32[256,1024]{1,0:T(8,128)S(1)}, f32[256,1024]{1,0:T(8,128)}, u32[]{:S(2)}) copy-start(f32[256,1024]{1,0:T(8,128)} %copy-done.5) | copy-start | bytes 3145732
  400.5 208.7 %reduce-scatter.21.cloned.1.call-start = ((), (), s32[]{:S(2)}) async-start(), calls=%async_computation.17 | async-start | bytes 1310720 | tf_op jit(solution)/shard_map/reduce_scatter | solution.py:242
  477.5 154.1 %reduce-scatter.31.cloned.1.call-start = ((), (), s32[]{:S(2)}) async-start(), calls=%async_computation.26 | async-start | bytes 163840
  482.7 18.8 %copy-start.41 = (bf16[1,16,256]{1,2,0:T(8,128)(2,1)S(1)}, bf16[1,16,256]{1,2,0:T(8,128)(2,1)}, u32[]{:S(2)}) copy-start(bf16[1,16,256]{1,2,0:T(8,128)(2,1)} %copy-done.40) | copy-start | bytes 24580
  482.7 18.8 %copy-start.43 = (bf16[1024,16]{0,1:T(8,128)(2,1)S(1)}, bf16[1024,16]{0,1:T(8,128)(2,1)}, u32[]{:S(2)}) copy-start(bf16[1024,16]{0,1:T(8,128)(2,1)} %copy-done.42) | copy-start | bytes 98308
  501.5 196.8 %all-reduce.10.cloned.1.call-start = ((), (), s32[]{:S(2)}) async-start(), calls=%async_computation.28 | async-start | bytes 4194304 | tf_op jit(solution)/shard_map/psum | solution.py:145
  502.8 106.5 %copy-start.56 = (f32[1024]{0:T(1024)S(1)}, f32[1024]{0:T(1024)}, u32[]{:S(2)}) copy-start(f32[1024]{0:T(1024)} %get-tuple-element.355) | copy-start | bytes 12292
  502.8 106.7 %copy-start.49 = (f32[1,1280]{1,0:T(1,128)S(1)}, f32[1,1280]{1,0:T(1,128)}, u32[]{:S(2)}) copy-start(f32[1,1280]{1,0:T(1,128)} %copy-done.48) | copy-start | bytes 15364
  502.8 106.7 %copy-start.51 = (f32[1,1280]{1,0:T(1,128)S(1)}, f32[1,1280]{1,0:T(1,128)}, u32[]{:S(2)}) copy-start(f32[1,1280]{1,0:T(1,128)} %copy-done.50) | copy-start | bytes 15364
  502.8 106.7 %copy-start.53 = (f32[1,1280]{1,0:T(1,128)S(1)}, f32[1,1280]{1,0:T(1,128)}, u32[]{:S(2)}) copy-start(f32[1,1280]{1,0:T(1,128)} %copy-done.52) | copy-start | bytes 15364
  502.8 106.7 %copy-start.55 = (f32[1,1280]{1,0:T(1,128)S(1)}, f32[1,1280]{1,0:T(1,128)}, u32[]{:S(2)}) copy-start(f32[1,1280]{1,0:T(1,128)} %copy-done.54) | copy-start | bytes 15364
  502.8 195.5 %copy-start.27 = (bf16[1024,256]{1,0:T(8,128)(2,1)S(1)}, bf16[1024,256]{1,0:T(8,128)(2,1)}, u32[]{:S(2)}) copy-start(bf16[1024,256]{1,0:T(8,128)(2,1)} %copy-done.26) | copy-start | bytes 1572868
  502.8 262.4 %reduce-scatter.25.cloned.1.call-start = ((), (), s32[]{:S(2)}) async-start(), calls=%async_computation.20 | async-start | bytes 327680 | tf_op jit(solution)/shard_map/reduce_scatter | solution.py:243
  528.1 244.2 %all-gather.19.cloned.1.call-start = ((), (), s32[]{:S(2)}) async-start(), calls=%async_computation.15 | async-start | bytes 1310720 | tf_op jit(solution)/shard_map/all_gather | solution.py:248
  554.4 217.9 %all-gather.23.cloned.1.call-start = ((), (), s32[]{:S(2)}) async-start(), calls=%async_computation.23 | async-start | bytes 1310720 | tf_op jit(solution)/shard_map/all_gather | solution.py:252
  581.6 194.9 %all-gather.21.cloned.1.call-start = ((), (), s32[]{:S(2)}) async-start(), calls=%async_computation.18 | async-start | bytes 1310720 | tf_op jit(solution)/shard_map/all_gather | solution.py:249
  698.3 64.1 %copy-start.28 = (bf16[1,256,1024]{2,1,0:T(8,128)(2,1)S(1)}, bf16[1,256,1024]{2,1,0:T(8,128)(2,1)}, u32[]{:S(2)}) copy-start(bf16[1,256,1024]{2,1,0:T(8,128)(2,1)} %param.39) | copy-start | bytes 1572868
  698.3 64.1 %copy-start.70 = (f32[256]{0:T(256)S(1)}, f32[256]{0:T(256)}, u32[]{:S(2)}) copy-start(f32[256]{0:T(256)} %get-tuple-element.376) | copy-start | bytes 3076
  (50 other events, 141.1 us)
Sparse Core Ops, SparseCore 0:
  9.6 56.9 all-gather.12
  80.3 23.7 all-gather.24
  105.7 45.9 all-gather.14
  153.1 44.9 all-gather.16
  218.4 20.8 all-gather.26
  241.5 76.7 reduce-scatter.14
  320.6 77.2 reduce-scatter.28
  400.2 77.2 reduce-scatter.18
  480.4 19.4 reduce-scatter.26
  502.7 25.3 reduce-scatter.22
  530.8 23.5 reduce-scatter.16
  556.7 24.8 reduce-scatter.32
  584.3 24.8 reduce-scatter.20
  612.1 19.5 reduce-scatter.30
  635.2 63.0 all-reduce.9
  700.6 20.0 reduce-scatter.24
  722.2 16.9 all-gather.18
  740.6 16.7 all-gather.22
  759.1 17.4 all-gather.20
where the time goes:
time: 796 us; the launch traced here: 787 us
  waiting for transfers between devices  466 us (59%)
  blocking collectives  142 us (18%)
  matrix products  71.4 us (9%)
  local copies, waits for them, and re-layouts  50.8 us (6%)
  other arithmetic  36.6 us (5%)
  between operations  15.3 us (2%)
    reduce_scatter x1, waiting for transfers between devices, on_device(): lax.psum_scatter(weight_grads[4], 'fsdp', scatter_dimension=1, tiled=True)  79.6 us
    reduce_scatter x1, waiting for transfers between devices, on_device(): lax.psum_scatter(weight_grads[1], 'fsdp', scatter_dimension=0, tiled=True)  77 us
    psum x1, blocking collectives, on_device(): lax.psum((grad_input_gain, grad_taps[:, :inner_here], grad_bc_conv, grad_...  62.2 us
    psum x1, waiting for transfers between devices, on_device(): lax.psum(jnp.dot(normed_out, full_out, preferred_element_type=jnp.float32...  59.9 us
    unnamed x21, waiting for transfers between devices  51.5 us
    all_gather x1, waiting for transfers between devices, on_device(): lax.all_gather(out_proj, 'fsdp', axis=1, tiled=True)  37.8 us
    all_gather x1, waiting for transfers between devices, on_device(): lax.all_gather(gate_proj, 'fsdp', axis=0, tiled=True)  36.8 us
    reduce_scatter x1, waiting for transfers between devices, on_device(): lax.psum_scatter(sectioned[1], 'ctx', scatter_dimension=0, tiled=True)  27.6 us
  transfers between devices with their start and end apart: 21, of which 17 were waited for; matrix products, arithmetic and copies ran while one was open for 16% of the time, Pallas kernels for 0%

commit v1 on v0

--- a/solution.py
+++ b/solution.py
@@ -252,16 +252,19 @@
         lax.all_gather(owned_rows[4], "ctx", axis=1, tiled=True),
     )
     small_totals = lax.psum(
-        (
-            grad_input_gain,
-            grad_taps[:, :inner_here],
-            grad_bc_conv,
-            grad_dt_bias,
-            grad_a_log,
-            grad_skip_gain,
-            grad_gated_gain,
+        lax.psum(
+            (
+                grad_input_gain,
+                grad_taps[:, :inner_here],
+                grad_bc_conv,
+                grad_dt_bias,
+                grad_a_log,
+                grad_skip_gain,
+                grad_gated_gain,
+            ),
+            "ctx",
         ),
-        ("fsdp", "ctx"),
+        "fsdp",
     )
     return (
         block_output,

time: 796 us -> 797 us (level)
  waiting for transfers between devices: 466 us -> 499 us
  blocking collectives: 142 us -> 110 us
    psum x1, blocking collectives: 62.2 us -> 11.4 us  [on_device(): lax.psum((grad_input_gain, grad_taps[:, :inner_here], grad_bc_conv, grad_...]
    psum x0 -> x1, blocking collectives: none -> 19.6 us  [on_device(): lax.psum(lax.psum((grad_input_gain, grad_taps[:, :inner_here], grad_bc_co...]
    all_gather x1, waiting for transfers between devices: 0.01 us -> 18.5 us  [on_device(): lax.all_gather(owned_rows[4], 'ctx', axis=1, tiled=True)]
    all_gather x1, waiting for transfers between devices: 1.64 us -> 15.9 us  [on_device(): lax.all_gather(owned_rows[1], 'ctx', axis=0, tiled=True)]
  transfers between devices with their start and end apart: 21 -> 21, of which waited for: 17 -> 18; matrix products, arithmetic and copies ran while one was open for 16% -> 16% of each run, Pallas kernels for 0% -> 0%
where the time goes in v1:
time: 797 us; the launch traced here: 787 us
  waiting for transfers between devices  499 us (63%)
  blocking collectives  110 us (14%)
  matrix products  71.4 us (9%)
  local copies, waits for them, and re-layouts  50.7 us (6%)
  other arithmetic  36.6 us (5%)
  between operations  15.3 us (2%)
    reduce_scatter x1, waiting for transfers between devices, on_device(): lax.psum_scatter(weight_grads[4], 'fsdp', scatter_dimension=1, tiled=True)  79.6 us
    reduce_scatter x1, waiting for transfers between devices, on_device(): lax.psum_scatter(weight_grads[1], 'fsdp', scatter_dimension=0, tiled=True)  77 us
    psum x1, waiting for transfers between devices, on_device(): lax.psum(jnp.dot(normed_out, full_out, preferred_element_type=jnp.float32...  59.9 us
    unnamed x21, waiting for transfers between devices  51.5 us
    all_gather x1, waiting for transfers between devices, on_device(): lax.all_gather(out_proj, 'fsdp', axis=1, tiled=True)  37.9 us
    all_gather x1, waiting for transfers between devices, on_device(): lax.all_gather(gate_proj, 'fsdp', axis=0, tiled=True)  36.8 us
    reduce_scatter x1, waiting for transfers between devices, on_device(): lax.psum_scatter(sectioned[1], 'ctx', scatter_dimension=0, tiled=True)  27.6 us
    reduce_scatter x1, waiting for transfers between devices, on_device(): lax.psum_scatter(sectioned[0], 'ctx', scatter_dimension=0, tiled=True)  26.2 us
  transfers between devices with their start and end apart: 21, of which 18 were waited for; matrix products, arithmetic and copies ran while one was open for 16% of the time, Pallas kernels for 0%

profile of v1, /device:TPU:0, one launch (start us, length us, event | category | flops | bytes accessed | tf_op | source)
XLA Modules:
  0.0 787.1 jit_solution(7739521720062136200)
XLA Ops:
  8.0 15.0 %all_gather.50 = bf16[1024,16]{0,1:T(8,128)(2,1)S(1)} all-gather(bf16[256,16]{0,1:T(8,128)(2,1)} %param.31), channel_id=1, replica_groups=mesh['fsdp'=4,'ctx'=4,'tp'=2] {'fsdp'}, dimensions={0}, use_global_device_ids=true | all-gather | bytes 40960 | tf_op jit(solution)/shard_map/all_gather | solution.py:95
  29.2 22.7 %all_gather.49 = bf16[1024,256]{1,0:T(8,128)(2,1)S(1)} all-gather(bf16[256,256]{1,0:T(8,128)(2,1)S(1)} %copy-done.44), channel_id=1, replica_groups=mesh['fsdp'=4,'ctx'=4,'tp'=2] {'fsdp'}, dimensions={0}, use_global_device_ids=true | all-gather | bytes 655360 | tf_op jit(solution)/shard_map/all_gather | solution.py:94
  54.0 12.6 %all-gather.13.cloned.1.call-done = bf16[1024,1024]{1,0:T(8,128)(2,1)} async-done(((bf16[256,1024]{1,0:T(8,128)(2,1)}), bf16[1024,1024]{1,0:T(8,128)(2,1)}) %all-gather.13.cloned.1.call-update) | async-done | bytes 2097168 | tf_op jit(solution)/shard_map/all_gather | solution.py:93
  77.2 2.9 fusion.62
  83.0 7.0 all-gather
  91.1 2.6 copy.207
  96.4 7.8 all-gather.25.cloned.1.call-done
  106.3 6.0 fusion.36
  112.3 2.6 copy.205
  114.9 36.8 %all-gather.15.cloned.1.call-done = bf16[1024,1024]{1,0:T(8,128)(2,1)} async-done(((bf16[256,1024]{1,0:T(8,128)(2,1)}), bf16[1024,1024]{1,0:T(8,128)(2,1)}) %all-gather.15.cloned.1.call-update) | async-done | bytes 2097168 | tf_op jit(solution)/shard_map/all_gather | solution.py:92
  151.7 3.7 multiply_reduce_fusion.8
  155.4 4.9 psum.140
  160.3 37.9 %all-gather.17.cloned.1.call-done = bf16[1024,1024]{1,0:T(8,128)(2,1)} async-done(((bf16[1024,256]{1,0:T(8,128)(2,1)}), bf16[1024,1024]{1,0:T(8,128)(2,1)}) %all-gather.17.cloned.1.call-update) | async-done | bytes 2097168 | tf_op jit(solution)/shard_map/all_gather | solution.py:96
  198.2 4.0 fusion.49
  202.2 5.4 psum.142
  207.6 2.9 fusion.59
  212.7 2.6 copy.208
  215.3 3.0 fusion.88
  221.5 2.8 fusion.121
  224.4 3.9 fusion.68
  228.4 2.6 copy.211
  231.0 8.6 %fusion.8 = (f32[16,256]{1,0:T(8,128)}, f32[16,256]{1,0:T(8,128)}, f32[16,256]{1,0:T(8,128)}, f32[256,256]{1,0:T(8,128)S(1)}) fusion(f32[16,256]{1,0:T(8,128)S(1)} %copy-done.57, f32[256,256]{1,0:T(8,128)} %fusion.92, f32[16,256]{1,0:T(8,128)S(1)} %copy-done.59, pred[256,256]{1,0:T(8,128)(4,1)} %iota_compare_fusion, f32[16,64,256]{2,1,0:T(8,128)} %bitcast.308, ...), kind=kOutput, calls=%fused_computation.20 | convolution fusion | flops 820957184 | bytes 2768896 | tf_op jit(solution)/shard_map/transpose(jvp(bhts,bshp->bthp))/dot_general | solution.py:49
  244.3 6.0 while.31
  252.8 4.9 fusion.30
  260.2 3.1 fusion.42
  263.4 2.6 multiply_reduce_fusion.5
  268.7 4.5 scatter-add.11
  275.8 4.4 scatter-add.14
  286.6 2.8 fusion.77
  300.4 12.9 %all-reduce.12 = (bf16[256,256]{1,0:T(8,128)(2,1)S(1)}, f32[4,256]{1,0:T(4,128)}) all-reduce(f32[256,256]{1,0:T(8,128)S(1)} %slice_bitcast_fusion, f32[4,256]{1,0:T(4,128)S(1)} %pad_maximum_fusion.2), channel_id=1, replica_groups=mesh['fsdp'=4,'ctx'=4,'tp'=2] {'tp'}, use_global_device_ids=true, to_apply=%region_24.25 | all-reduce | flops 66560 | bytes 401408 | tf_op jit(solution)/shard_map/psum | solution.py:199
  314.8 3.4 reduce-scatter.15.cloned.1.call-done
  318.4 79.6 %reduce-scatter.29.cloned.1.call-done = f32[1024,256]{1,0:T(8,128)} async-done(((f32[1024,1024]{1,0:T(8,128)}), f32[1024,256]{1,0:T(8,128)}) %reduce-scatter.29.cloned.1.call-update) | async-done | bytes 1048592 | tf_op jit(solution)/shard_map/reduce_scatter | solution.py:238
  400.6 77.0 %reduce-scatter.19.cloned.1.call-done = f32[256,1024]{1,0:T(8,128)} async-done(((f32[1024,1024]{1,0:T(8,128)}), f32[256,1024]{1,0:T(8,128)}) %reduce-scatter.19.cloned.1.call-update) | async-done | bytes 1048592 | tf_op jit(solution)/shard_map/reduce_scatter | solution.py:235
  477.7 3.5 convolution_bitcast_fusion
  483.5 16.5 %reduce-scatter.27.cloned.1.call-done = f32[256,16]{0,1:T(8,128)} async-done(((f32[1024,16]{0,1:T(8,128)}), f32[256,16]{0,1:T(8,128)}) %reduce-scatter.27.cloned.1.call-update) | async-done | bytes 16400 | tf_op jit(solution)/shard_map/reduce_scatter | solution.py:237
  502.9 25.2 %reduce-scatter.23.cloned.1.call-done = f32[256,256]{1,0:T(8,128)} async-done(((f32[1024,256]{1,0:T(8,128)}), f32[256,256]{1,0:T(8,128)}) %reduce-scatter.23.cloned.1.call-update) | async-done | bytes 262160 | tf_op jit(solution)/shard_map/reduce_scatter | solution.py:236
  528.2 26.2 %reduce-scatter.17.cloned.1.call-done = f32[64,1024]{1,0:T(8,128)} async-done(((f32[256,1024]{1,0:T(8,128)}), f32[64,1024]{1,0:T(8,128)}) %reduce-scatter.17.cloned.1.call-update) | async-done | bytes 262160 | tf_op jit(solution)/shard_map/reduce_scatter | solution.py:241
  554.5 27.2 %reduce-scatter.33.cloned.1.call-done = f32[64,1024]{1,0:T(8,128)} async-done(((f32[256,1024]{1,0:T(8,128)}), f32[64,1024]{1,0:T(8,128)}) %reduce-scatter.33.cloned.1.call-update) | async-done | bytes 262160
  581.8 27.6 %reduce-scatter.21.cloned.1.call-done = f32[64,1024]{1,0:T(8,128)} async-done(((f32[256,1024]{1,0:T(8,128)}), f32[64,1024]{1,0:T(8,128)}) %reduce-scatter.21.cloned.1.call-update) | async-done | bytes 262160 | tf_op jit(solution)/shard_map/reduce_scatter | solution.py:242
  609.6 22.1 %reduce-scatter.31.cloned.1.call-done = f32[64,16]{1,0:T(8,128)} async-done(((f32[256,16]{1,0:T(8,128)}), f32[64,16]{1,0:T(8,128)}) %reduce-scatter.31.cloned.1.call-update) | async-done | bytes 4112
  632.6 5.2 all-gather.3
  638.5 59.9 %all-reduce.11.cloned.1.call-done = (f32[1,256,1024]{2,1,0:T(8,128)}, f32[256,1024]{1,0:T(8,128)}) async-done(((f32[1,256,1024]{2,1,0:T(8,128)}, f32[256,1024]{1,0:T(8,128)}), (f32[1,256,1024]{2,1,0:T(8,128)}, f32[256,1024]{1,0:T(8,128)})) %all-reduce.11.cloned.1.call-update) | async-done | bytes 2097168 | tf_op jit(solution)/shard_map/psum | solution.py:145
  700.3 11.4 %all-reduce.4 = (f32[1024]{0:T(1024)S(1)}, f32[4,1024]{1,0:T(4,128)S(1)}, f32[4,256]{1,0:T(4,128)S(1)}, f32[16]{0:T(128)S(1)}, f32[16]{0:T(128)S(1)}, /*index=5*/f32[16]{0:T(128)S(1)}, f32[1024]{0:T(1024)S(1)}) all-reduce(f32[1024]{0:T(1024)S(1)} %get-tuple-element.317, ...), channel_id=1, replica_groups=mesh['fsdp'=4,'ctx'=4,'tp'=2] {'ctx'}, use_global_device_ids=true, to_apply=%region_27.28 | all-reduce | flops 7216 | bytes 57728 | tf_op jit(solution)/shard_map/psum | solution.py:255
  711.8 19.6 %all-reduce.5 = (f32[1024]{0:T(1024)}, f32[4,1024]{1,0:T(4,128)}, f32[4,256]{1,0:T(4,128)}, f32[16]{0:T(128)}, f32[16]{0:T(128)}, /*index=5*/f32[16]{0:T(128)}, f32[1024]{0:T(1024)}) all-reduce(f32[1024]{0:T(1024)S(1)} %get-tuple-element.344, ...), channel_id=1, replica_groups=mesh['fsdp'=4,'ctx'=4,'tp'=2] {'fsdp'}, use_global_device_ids=true, to_apply=%region_28.29 | all-reduce | flops 7216 | bytes 57728 | tf_op jit(solution)/shard_map/psum | solution.py:254
  731.4 2.8 fusion.55
  734.1 6.0 all_gather.60
  740.1 18.5 %all-gather.23.cloned.1.call-done = f32[1024,256]{0,1:T(8,128)} async-done(((f32[1024,64]{0,1:T(8,128)}), f32[1024,256]{0,1:T(8,128)}) %all-gather.23.cloned.1.call-update) | async-done | bytes 1048592 | tf_op jit(solution)/shard_map/all_gather | solution.py:252
  761.2 15.9 %all-gather.21.cloned.1.call-done = f32[256,1024]{1,0:T(8,128)} async-done(((f32[64,1024]{1,0:T(8,128)}), f32[256,1024]{1,0:T(8,128)}) %all-gather.21.cloned.1.call-update) | async-done | bytes 1048592 | tf_op jit(solution)/shard_map/all_gather | solution.py:249
  (304 shorter events, 90.4 us)
Async XLA Ops:
  7.2 59.4 %all-gather.13.cloned.1.call-start = ((), (), s32[]{:S(2)}) async-start(), calls=%async_computation.10 | async-start | bytes 2621440 | tf_op jit(solution)/shard_map/all_gather | solution.py:93
  7.9 96.3 %all-gather.25.cloned.1.call-start = ((), (), s32[]{:S(2)}) async-start(), calls=%async_computation.24 | async-start | bytes 2621440 | tf_op jit(solution)/shard_map/all_gather | solution.py:20
  26.0 26.7 %copy-start.2 = (bf16[1,256,1024]{2,1,0:T(8,128)(2,1)S(1)}, bf16[1,256,1024]{2,1,0:T(8,128)(2,1)}, u32[]{:S(2)}) copy-start(bf16[1,256,1024]{2,1,0:T(8,128)(2,1)} %param.26) | copy-start | bytes 1572868
  26.0 26.7 %copy-start.37 = (f32[1024]{0:T(1024)S(1)}, f32[1024]{0:T(1024)}, u32[]{:S(2)}) copy-start(f32[1024]{0:T(1024)} %param.27) | copy-start | bytes 12292
  27.6 25.6 %copy-start.33 = (f32[1,16,256]{1,2,0:T(8,128)}, f32[1,16,256]{1,2,0:T(8,128)S(1)}, u32[]{:S(2)}) copy-start(f32[1,16,256]{1,2,0:T(8,128)S(1)} %get-tuple-element.387) | copy-start | bytes 49156
  27.6 25.6 %copy-start.29 = (f32[1,16,256]{1,2,0:T(8,128)}, f32[1,16,256]{1,2,0:T(8,128)S(1)}, u32[]{:S(2)}) copy-start(f32[1,16,256]{1,2,0:T(8,128)S(1)} %get-tuple-element.388) | copy-start | bytes 49156
  29.2 24.0 %copy-start.24 = (f32[1,16,256]{1,2,0:T(8,128)}, f32[1,16,256]{1,2,0:T(8,128)S(1)}, u32[]{:S(2)}) copy-start(f32[1,16,256]{1,2,0:T(8,128)S(1)} %get-tuple-element.372) | copy-start | bytes 49156
  53.2 18.5 %copy-start.21 = (f32[1,256,256]{2,1,0:T(8,128)}, f32[1,256,256]{2,1,0:T(8,128)S(1)}, u32[]{:S(2)}) copy-start(f32[1,256,256]{2,1,0:T(8,128)S(1)} %convolution_bitcast_fusion.3) | copy-start | bytes 786436
  53.2 15.8 %copy-start.65 = (f32[16]{0:T(128)}, f32[16]{0:T(128)S(1)}, u32[]{:S(2)}) copy-start(f32[16]{0:T(128)S(1)} %get-tuple-element.381) | copy-start | bytes 196
  69.0 2.6 collective-permute-start
  77.2 29.0 %copy-start.7 = (f32[1,256,1024]{1,2,0:T(8,128)}, f32[1,256,1024]{1,2,0:T(8,128)S(1)}, u32[]{:S(2)}) copy-start(f32[1,256,1024]{1,2,0:T(8,128)S(1)} %copy.193) | copy-start | bytes 3145732
  80.2 9.8 %copy-start.35 = (f32[256,16]{1,0:T(8,128)S(1)}, f32[256,16]{1,0:T(8,128)}, u32[]{:S(2)}) copy-start(f32[256,16]{1,0:T(8,128)} %get-tuple-element.371) | copy-start | bytes 49156
  80.2 71.5 %all-gather.15.cloned.1.call-start = ((), (), s32[]{:S(2)}) async-start(), calls=%async_computation.11 | async-start | bytes 2621440 | tf_op jit(solution)/shard_map/all_gather | solution.py:92
  80.9 117.2 %all-gather.17.cloned.1.call-start = ((), (), s32[]{:S(2)}) async-start(), calls=%async_computation.12 | async-start | bytes 2621440 | tf_op jit(solution)/shard_map/all_gather | solution.py:96
  81.5 162.7 %all-gather.27.cloned.1.call-start = ((), (), s32[]{:S(2)}) async-start(), calls=%async_computation.25 | async-start | bytes 2621440 | tf_op jit(solution)/shard_map/all_gather | solution.py:20
  104.2 8.1 %copy-start.73 = (f32[4,1,16]{2,1,0:T(1,128)}, f32[4,1,16]{2,1,0:T(1,128)S(1)}, u32[]{:S(2)}) copy-start(f32[4,1,16]{2,1,0:T(1,128)S(1)} %get-tuple-element.628) | copy-start | bytes 772
  114.9 83.3 %copy-start.45 = (f32[1024]{0:T(1024)S(1)}, f32[1024]{0:T(1024)}, u32[]{:S(2)}) copy-start(f32[1024]{0:T(1024)} %param.37) | copy-start | bytes 12292
  155.4 69.0 %copy-start.5 = (f32[256,1024]{1,0:T(8,128)}, f32[256,1024]{1,0:T(8,128)S(1)}, u32[]{:S(2)}) copy-start(f32[256,1024]{1,0:T(8,128)S(1)} %get-tuple-element.370) | copy-start | bytes 3145732
  218.4 99.9 %reduce-scatter.15.cloned.1.call-start = ((), (), s32[]{:S(2)}) async-start(), calls=%async_computation.13 | async-start | bytes 5242880 | tf_op jit(solution)/shard_map/reduce_scatter | solution.py:234
  224.3 173.7 %reduce-scatter.29.cloned.1.call-start = ((), (), s32[]{:S(2)}) async-start(), calls=%async_computation.22 | async-start | bytes 5242880 | tf_op jit(solution)/shard_map/reduce_scatter | solution.py:238
  228.3 249.3 %reduce-scatter.19.cloned.1.call-start = ((), (), s32[]{:S(2)}) async-start(), calls=%async_computation.16 | async-start | bytes 5242880 | tf_op jit(solution)/shard_map/reduce_scatter | solution.py:235
  231.0 10.1 %copy-start.13 = (f32[256,1024]{0,1:T(8,128)S(1)}, f32[256,1024]{0,1:T(8,128)}, u32[]{:S(2)}) copy-start(f32[256,1024]{0,1:T(8,128)} %copy.208) | copy-start | bytes 3145732
  281.0 3.1 collective-permute-start.1
  289.5 210.5 %reduce-scatter.27.cloned.1.call-start = ((), (), s32[]{:S(2)}) async-start(), calls=%async_computation.21 | async-start | bytes 81920 | tf_op jit(solution)/shard_map/reduce_scatter | solution.py:237
  293.1 7.2 copy-start.11
  299.3 15.4 %copy-start.40 = (bf16[1,16,256]{1,2,0:T(8,128)(2,1)}, bf16[1,16,256]{1,2,0:T(8,128)(2,1)S(1)}, u32[]{:S(2)}) copy-start(bf16[1,16,256]{1,2,0:T(8,128)(2,1)S(1)} %get-tuple-element.365) | copy-start | bytes 24580
  300.3 227.8 %reduce-scatter.23.cloned.1.call-start = ((), (), s32[]{:S(2)}) async-start(), calls=%async_computation.19 | async-start | bytes 1310720 | tf_op jit(solution)/shard_map/reduce_scatter | solution.py:236
  314.8 239.6 %reduce-scatter.17.cloned.1.call-start = ((), (), s32[]{:S(2)}) async-start(), calls=%async_computation.14 | async-start | bytes 1310720 | tf_op jit(solution)/shard_map/reduce_scatter | solution.py:241
  318.3 263.4 %reduce-scatter.33.cloned.1.call-start = ((), (), s32[]{:S(2)}) async-start(), calls=%async_computation.27 | async-start | bytes 1310720
  400.5 77.1 %copy-start.6 = (f32[256,1024]{1,0:T(8,128)S(1)}, f32[256,1024]{1,0:T(8,128)}, u32[]{:S(2)}) copy-start(f32[256,1024]{1,0:T(8,128)} %copy-done.5) | copy-start | bytes 3145732
  400.6 208.8 %reduce-scatter.21.cloned.1.call-start = ((), (), s32[]{:S(2)}) async-start(), calls=%async_computation.17 | async-start | bytes 1310720 | tf_op jit(solution)/shard_map/reduce_scatter | solution.py:242
  477.6 154.2 %reduce-scatter.31.cloned.1.call-start = ((), (), s32[]{:S(2)}) async-start(), calls=%async_computation.26 | async-start | bytes 163840
  482.7 18.8 %copy-start.41 = (bf16[1,16,256]{1,2,0:T(8,128)(2,1)S(1)}, bf16[1,16,256]{1,2,0:T(8,128)(2,1)}, u32[]{:S(2)}) copy-start(bf16[1,16,256]{1,2,0:T(8,128)(2,1)} %copy-done.40) | copy-start | bytes 24580
  482.8 18.8 %copy-start.43 = (bf16[1024,16]{0,1:T(8,128)(2,1)S(1)}, bf16[1024,16]{0,1:T(8,128)(2,1)}, u32[]{:S(2)}) copy-start(bf16[1024,16]{0,1:T(8,128)(2,1)} %copy-done.42) | copy-start | bytes 98308
  501.5 196.8 %all-reduce.11.cloned.1.call-start = ((), (), s32[]{:S(2)}) async-start(), calls=%async_computation.28 | async-start | bytes 4194304 | tf_op jit(solution)/shard_map/psum | solution.py:145
  502.8 106.5 %copy-start.56 = (f32[1024]{0:T(1024)S(1)}, f32[1024]{0:T(1024)}, u32[]{:S(2)}) copy-start(f32[1024]{0:T(1024)} %get-tuple-element.362) | copy-start | bytes 12292
  502.8 106.7 %copy-start.49 = (f32[1,1280]{1,0:T(1,128)S(1)}, f32[1,1280]{1,0:T(1,128)}, u32[]{:S(2)}) copy-start(f32[1,1280]{1,0:T(1,128)} %copy-done.48) | copy-start | bytes 15364
  502.8 106.7 %copy-start.51 = (f32[1,1280]{1,0:T(1,128)S(1)}, f32[1,1280]{1,0:T(1,128)}, u32[]{:S(2)}) copy-start(f32[1,1280]{1,0:T(1,128)} %copy-done.50) | copy-start | bytes 15364
  502.8 106.7 %copy-start.53 = (f32[1,1280]{1,0:T(1,128)S(1)}, f32[1,1280]{1,0:T(1,128)}, u32[]{:S(2)}) copy-start(f32[1,1280]{1,0:T(1,128)} %copy-done.52) | copy-start | bytes 15364
  502.9 106.7 %copy-start.55 = (f32[1,1280]{1,0:T(1,128)S(1)}, f32[1,1280]{1,0:T(1,128)}, u32[]{:S(2)}) copy-start(f32[1,1280]{1,0:T(1,128)} %copy-done.54) | copy-start | bytes 15364
  502.9 195.5 %copy-start.27 = (bf16[1024,256]{1,0:T(8,128)(2,1)S(1)}, bf16[1024,256]{1,0:T(8,128)(2,1)}, u32[]{:S(2)}) copy-start(bf16[1024,256]{1,0:T(8,128)(2,1)} %copy-done.26) | copy-start | bytes 1572868
  502.9 231.2 %reduce-scatter.25.cloned.1.call-start = ((), (), s32[]{:S(2)}) async-start(), calls=%async_computation.20 | async-start | bytes 327680 | tf_op jit(solution)/shard_map/reduce_scatter | solution.py:243
  528.2 212.0 %all-gather.19.cloned.1.call-start = ((), (), s32[]{:S(2)}) async-start(), calls=%async_computation.15 | async-start | bytes 1310720 | tf_op jit(solution)/shard_map/all_gather | solution.py:248
  554.4 204.3 %all-gather.23.cloned.1.call-start = ((), (), s32[]{:S(2)}) async-start(), calls=%async_computation.23 | async-start | bytes 1310720 | tf_op jit(solution)/shard_map/all_gather | solution.py:252
  581.7 195.3 %all-gather.21.cloned.1.call-start = ((), (), s32[]{:S(2)}) async-start(), calls=%async_computation.18 | async-start | bytes 1310720 | tf_op jit(solution)/shard_map/all_gather | solution.py:249
  698.4 33.0 %copy-start.28 = (bf16[1,256,1024]{2,1,0:T(8,128)(2,1)S(1)}, bf16[1,256,1024]{2,1,0:T(8,128)(2,1)}, u32[]{:S(2)}) copy-start(bf16[1,256,1024]{2,1,0:T(8,128)(2,1)} %param.39) | copy-start | bytes 1572868
  698.4 33.0 %copy-start.70 = (f32[256]{0:T(256)S(1)}, f32[256]{0:T(256)}, u32[]{:S(2)}) copy-start(f32[256]{0:T(256)} %get-tuple-element.383) | copy-start | bytes 3076
  740.1 36.9 %copy-start.31 = (f32[256,1024]{1,0:T(8,128)S(1)}, f32[256,1024]{1,0:T(8,128)}, u32[]{:S(2)}) copy-start(f32[256,1024]{1,0:T(8,128)} %all-gather.19.cloned.1.call-done) | copy-start | bytes 3145732
  (50 other events, 143.0 us)
Sparse Core Ops, SparseCore 0:
  9.6 56.9 all-gather.12
  80.3 23.7 all-gather.24
  105.7 45.9 all-gather.14
  153.1 45.0 all-gather.16
  218.5 20.8 all-gather.26
  241.5 76.7 reduce-scatter.14
  320.7 77.2 reduce-scatter.28
  400.3 77.2 reduce-scatter.18
  480.5 19.5 reduce-scatter.26
  502.7 25.3 reduce-scatter.22
  530.8 23.5 reduce-scatter.16
  556.8 24.8 reduce-scatter.32
  584.4 24.8 reduce-scatter.20
  612.2 19.5 reduce-scatter.30
  635.2 63.0 all-reduce.10
  700.7 20.0 reduce-scatter.24
  722.3 17.1 all-gather.18
  741.0 17.6 all-gather.22
  760.3 16.7 all-gather.20
